TPU v7x, 128 devices: a whole 4x4x4 slice. The times are simulated.
128 devices in a mesh: pole: 4 (over y_lo, core), dom: 32 (over z, x, y_hi).
Axes of the slice: x: 4, y: 4 (y_hi: 2, y_lo: 2; y = y_hi * 2 + y_lo), z: 4, core: 2. Of those that a mesh axis runs over, the one named last changes fastest.
Arguments:
- initial_block: bfloat16 [32, 8, 512, 256], P('dom'), may hold values from -24 to 24
- coupling: bfloat16 [32, 8, 512, 512], P('dom'), may hold values from -0.125 to 0.125
- pivots: bfloat16 [4, 32, 8, 2, 512, 512], P('pole', 'dom'), may hold values from -0.125 to 0.125
- interface: bfloat16 [4, 32, 3, 2, 512, 512], P('pole', 'dom'), may hold values from -0.1875 to 0.1875
- pole_values: float32 [4, 4], P('pole'), may hold values from 0.5 to 1.5
Outputs:
- filtered_basis: float32 [32, 8, 512, 256], P('dom', 'pole')
- rayleigh: float32 [256, 256], replicated
All inputs are finite; a program needn't handle non-finite values.
Results may differ from a plain program's by a relative error of at most 0.008.
Values sent between devices are 32-bit elements; how exact they have to be, the bound alone decides.
A program may use at most 192 MiB of HBM per device.

v0:
```python
import jax
import jax.numpy as jnp
from jax import lax
from jax.sharding import PartitionSpec as P

B = 512
M = 256


def shifted(x, axis, by):
    length = lax.axis_size(axis)
    pairs = [(i, i + by) for i in range(length) if 0 <= i + by < length]
    return lax.ppermute(x, axis, pairs)


def lower_solve(factor, right_side):
    return lax.linalg.triangular_solve(factor, right_side, left_side=True, lower=True)


def complex_product(matrix, vectors):
    block_order = matrix.shape[1]
    half_width = vectors.shape[1] // 2
    stacked = matrix.reshape(2 * block_order, block_order)
    stacked_out = jnp.dot(stacked, vectors.astype(jnp.bfloat16), preferred_element_type=jnp.float32)
    real_part = stacked_out[:block_order, :half_width] - stacked_out[block_order:, half_width:]
    imag_part = stacked_out[:block_order, half_width:] + stacked_out[block_order:, :half_width]
    return jnp.concatenate([real_part, imag_part], axis=1)


def real_product(matrix, vectors):
    return jnp.dot(matrix, vectors.astype(jnp.bfloat16), preferred_element_type=jnp.float32)


def transposed_product(matrix, vectors):
    return lax.dot_general(
        matrix,
        vectors.astype(jnp.bfloat16),
        (((0,), (0,)), ((), ())),
        preferred_element_type=jnp.float32,
    )


def inner_products(left, right_side):
    return lax.dot_general(
        left,
        right_side,
        (((0,), (0,)), ((), ())),
        precision=lax.Precision.HIGHEST,
        preferred_element_type=jnp.float32,
    )


def partition_solve(inverse, coupled, source):
    previous = jnp.roll(coupled, 1, axis=0)
    initial = jnp.zeros(source.shape[1:], jnp.float32)

    def forward_step(carried, members):
        block_inverse, given, couple_prev = members
        result = complex_product(block_inverse, given + transposed_product(couple_prev, carried))
        return (result, result)

    unused, forward = lax.scan(forward_step, initial, (inverse, source, previous))

    def backward_step(carried, members):
        block_inverse, partial_value, couple_next = members
        result = partial_value + complex_product(block_inverse, real_product(couple_next, carried))
        return (result, result)

    unused, backward = lax.scan(backward_step, initial, (inverse, forward, coupled), reverse=True)
    return backward


def on_device(initial_block, coupling, pivots, interface, pole_values):
    blocks = coupling.shape[1]
    coupled = coupling[0]
    inverse = pivots[0, 0]
    factors = interface[0, 0]
    real_start = initial_block[0].astype(jnp.float32)
    source = jnp.concatenate([real_start, jnp.zeros_like(real_start)], axis=-1)
    first = partition_solve(inverse, coupled, source)
    bottom = first[blocks - 1]
    top = first[0]
    top_next = shifted(top, "dom", -1)
    below = complex_product(factors[0], bottom) - complex_product(factors[1], top_next)
    topmost = lax.axis_index("dom") == lax.axis_size("dom") - 1
    above = jnp.where(
        topmost, jnp.zeros_like(top_next), top_next - complex_product(factors[2], below)
    )
    link = coupled[blocks - 1]
    lifted = transposed_product(link, below)
    arriving = shifted(lifted, "dom", 1)
    update = source.at[0].add(arriving)
    update = update.at[blocks - 1].add(real_product(link, above))
    second = partition_solve(inverse, coupled, update)
    real_z = pole_values[0, 0]
    imag_z = pole_values[0, 1]
    real_w = pole_values[0, 2]
    imag_w = pole_values[0, 3]
    real_x = second[..., :M]
    imag_x = second[..., M:]
    filtered_term = real_w * real_x - imag_w * imag_x
    shifted_term = (
        (real_w * real_z - imag_w * imag_z) * real_x
        - (real_w * imag_z + imag_w * real_z) * imag_x
        - real_w * real_start
    )
    count = blocks // lax.axis_size("pole")
    owned, shifted_owned = (
        lax.psum_scatter(filtered_term[None], "pole", scatter_dimension=1, tiled=True),
        lax.psum_scatter(shifted_term[None], "pole", scatter_dimension=1, tiled=True),
    )
    own_rows = owned[0].reshape(count * B, M)
    gram_part = inner_products(own_rows, own_rows)
    projected_part = inner_products(own_rows, shifted_owned[0].reshape(count * B, M))
    gram_total, projected_total = lax.psum((gram_part, projected_part), ("pole", "dom"))
    row_total = blocks * B * lax.axis_size("dom")
    gram = gram_total / row_total
    projected = projected_total / row_total
    factor = jnp.linalg.cholesky(gram)
    filtered_basis = lower_solve(factor, own_rows.T).T.reshape(1, count, B, M)
    middle = lower_solve(factor, projected)
    rayleigh = lower_solve(factor, middle.T).T
    return (filtered_basis, rayleigh)


def solution(mesh):
    in_specs = (
        P("dom", None, None, None),
        P("dom", None, None, None),
        P("pole", "dom", None, None, None, None),
        P("pole", "dom", None, None, None, None),
        P("pole", None),
    )
    out_specs = (P("dom", "pole", None, None), P())
    return jax.shard_map(
        on_device, mesh=mesh, in_specs=in_specs, out_specs=out_specs, check_vma=False
    )
```

profile of v0, /device:TPU:1, one launch (start us, length us, event | category | flops | bytes accessed | tf_op | source)
XLA Modules:
  0.0 714.1 jit_solution(7158494593496729926)
XLA Ops:
  7.2 4.2 slice_bitcast_fusion
  12.5 2.9 copy.17
  18.0 4.2 concatenate.76
  22.3 2.3 pad_maximum_fusion.2
  24.6 4.3 broadcast.158.clone.2
  29.7 65.3 %while.65 = (s32[]{:T(128)}, bf16[512,512]{0,1:T(8,128)(2,1)}, f32[8,512,512]{1,2,0:T(8,128)}, bf16[8,2,512,512]{3,2,1,0:T(8,128)(2,1)}, f32[8,512,512]{1,2,0:T(8,128)}, /*index=5*/bf16[8,512,512]{2,1,0:T(8,128)(2,1)}, s32[]{:T(128)}) while((s32[]{:T(128)}, bf16[512,512]{0,1:T(8,128)(2,1)}, f32[8,512,512]{1,2,0:T(8,128)}, ...), condition=%wide.region_1.2_spmd, body=%wide.region_0.1_spmd.sunk | while | flops 806617088 | bytes 17302612 | solution.py:62
  33.6 2.7 fusion.131
  41.8 2.7 fusion.131
  50.0 2.7 fusion.131
  58.1 2.7 fusion.131
  66.3 2.7 fusion.131
  74.5 2.7 fusion.131
  82.6 2.7 fusion.131
  90.8 2.7 fusion.131
  95.0 4.3 broadcast.158.clone.1
  99.3 67.7 %while.68 = (s32[]{:T(128)}, bf16[512,512]{0,1:T(8,128)(2,1)}, f32[8,512,512]{1,2,0:T(8,128)}, f32[8,512,512]{1,2,0:T(8,128)}, bf16[8,2,512,512]{3,2,1,0:T(8,128...) while((s32[]{:T(128)}, bf16[512,512]{0,1:T(8,128)(2,1)}, ...), condition=%wide.region_3.4_spmd.clone, body=%wide.region_2.3_spmd.clone.sunk | while | flops 807403520 | bytes 15204483 | solution.py:69
  103.0 2.5 fusion.140
  109.0 2.3 fusion.139
  111.5 2.4 fusion.140
  120.0 2.4 fusion.140
  128.5 2.4 fusion.140
  136.9 2.4 fusion.140
  145.4 2.4 fusion.140
  153.9 2.4 fusion.140
  162.4 2.4 fusion.140
  173.9 22.7 %collective-permute-done = f32[512,512]{0,1:T(8,128)S(1)} collective-permute-done((f32[512,512]{0,1:T(8,128)S(1)}, f32[512,512]{0,1:T(8,128)S(1)}, u32[]{:S(2)}, u32[]{:S(2)}) %collective-permute-start) | collective-permute-done | bytes 1048608 | tf_op jit(solution)/shard_map/ppermute | solution.py:13
  197.8 2.5 convolution_bitcast_fusion.4
  200.3 7.2 %collective-permute-start.1 = (f32[512,512]{0,1:T(8,128)}, f32[512,512]{0,1:T(8,128)}, u32[]{:S(2)}, u32[]{:S(2)}) collective-permute-start(f32[512,512]{0,1:T(8,128)} %convolution_bitcast_fusion.4), channel_id=1, source_target_pairs={{0,1},{1,2},{2,3},{3,4},{4,5},{5,6},{6,7},{7,8},{8,9},{9,10},{10,1... | collective-permute-start | bytes 3145736 | tf_op jit(solution)/shard_map/ppermute | solution.py:13
  213.9 13.3 %collective-permute-done.1 = f32[512,512]{0,1:T(8,128)} collective-permute-done((f32[512,512]{0,1:T(8,128)}, f32[512,512]{0,1:T(8,128)}, u32[]{:S(2)}, u32[]{:S(2)}) %collective-permute-start.1) | collective-permute-done | bytes 1048608 | tf_op jit(solution)/shard_map/ppermute | solution.py:13
  227.2 2.3 fusion.51
  229.5 2.9 fusion.52
  232.4 4.3 broadcast.158.clone
  237.6 65.4 %while.66 = (s32[]{:T(128)}, bf16[512,512]{0,1:T(8,128)(2,1)}, f32[8,512,512]{1,2,0:T(8,128)}, bf16[8,2,512,512]{3,2,1,0:T(8,128)(2,1)}, f32[8,512,512]{1,2,0:T(8,128)}, /*index=5*/bf16[8,512,512]{2,1,0:T(8,128)(2,1)}, s32[]{:T(128)}) while((s32[]{:T(128)}, bf16[512,512]{0,1:T(8,128)(2,1)}, f32[8,512,512]{1,2,0:T(8,128)}, ...), condition=%wide.region_5.6_spmd, body=%wide.region_4.5_spmd.sunk | while | flops 806617088 | bytes 17302612 | solution.py:62
  241.5 2.7 fusion.135
  249.7 2.7 fusion.135
  257.8 2.7 fusion.135
  266.0 2.7 fusion.135
  274.2 2.7 fusion.135
  282.5 2.7 fusion.135
  290.6 2.7 fusion.135
  298.8 2.7 fusion.135
  303.0 4.3 broadcast.158
  307.4 67.7 %while.69 = (s32[]{:T(128)}, bf16[512,512]{0,1:T(8,128)(2,1)}, f32[8,512,512]{1,2,0:T(8,128)}, f32[8,512,512]{1,2,0:T(8,128)}, bf16[8,2,512,512]{3,2,1,0:T(8,128...) while((s32[]{:T(128)}, bf16[512,512]{0,1:T(8,128)(2,1)}, ...), condition=%wide.region_7.8_spmd.clone, body=%wide.region_6.7_spmd.clone.sunk | while | flops 807403520 | bytes 15204483 | solution.py:69
  311.1 2.5 fusion.144
  317.0 2.3 fusion.143
  319.6 2.4 fusion.144
  328.0 2.4 fusion.144
  336.5 2.4 fusion.144
  345.0 2.4 fusion.144
  350.9 2.3 fusion.143
  353.5 2.4 fusion.144
  361.9 2.4 fusion.144
  370.4 2.4 fusion.144
  375.0 9.9 %subtract_bitcast_fusion = (f32[1,8,512,256]{2,3,1,0:T(8,128)}, f32[1,8,512,256]{2,3,1,0:T(8,128)}) fusion(f32[8,512,512]{1,2,0:T(8,128)} %get-tuple-element.338, f32[]{:T(128)S(6)} %add.169, f32[]{:T(128)S(6)} %sub.71, f32[]{:T(128)} %bitcast.8, bf16[1,8,512,256]{2,3,1,0:T(8,128)(2,1)} %copy-done.2, f32[]{:T(128)} %bitcast.27), kind=kLoop, calls=%fused_computation.61 | loop fusion | flops 9437184 | bytes 18874384 | tf_op jit(solution)/shard_map/broadcast_in_dim | solution.py:110
  386.0 51.5 %reduce-scatter.3.cloned.1.call-done = f32[1,2,512,256]{2,3,1,0:T(8,128)} async-done(((f32[1,8,512,256]{2,3,1,0:T(8,128)}), f32[1,2,512,256]{2,3,1,0:T(8,128)}) %reduce-scatter.3.cloned.1.call-update) | async-done | bytes 1048592 | tf_op jit(solution)/shard_map/reduce_scatter | solution.py:109
  437.4 3.4 convolution_bitcast_fusion.6
  440.8 45.5 %reduce-scatter.5.cloned.1.call-done = f32[1,2,512,256]{2,3,1,0:T(8,128)} async-done(((f32[1,8,512,256]{2,3,1,0:T(8,128)}), f32[1,2,512,256]{2,3,1,0:T(8,128)}) %reduce-scatter.5.cloned.1.call-update) | async-done | bytes 1048592 | tf_op jit(solution)/shard_map/reduce_scatter | solution.py:110
  486.3 3.3 convolution_bitcast_fusion.5
  490.0 148.1 %all-reduce.5.cloned.1.call-done = (f32[256,256]{0,1:T(8,128)}, f32[256,256]{0,1:T(8,128)}) async-done(((f32[256,256]{0,1:T(8,128)}, f32[256,256]{0,1:T(8,128)}), (f32[256,256]{0,1:T(8,128)}, f32[256,256]{0,1:T(8,128)})) %all-reduce.5.cloned.1.call-update) | async-done | bytes 524304 | tf_op jit(solution)/shard_map/psum | solution.py:115
  640.3 11.7 %cholesky.50 = f32[128,128]{1,0:T(8,128)S(1)} custom-call(f32[128,128]{1,0:T(8,128)S(1)} %cholesky.118), custom_call_target="Cholesky" | custom-call | tf_op jit(solution)/shard_map/jit(cholesky)/cholesky | solution.py:119
  652.1 9.8 %custom-call.17 = f32[1,128,128]{1,2,0:T(8,128)S(1)} custom-call(f32[1,128,128]{2,1,0:T(8,128)S(1)} %get-tuple-element.519), custom_call_target="InvertDiagBlocksLowerTriangular" | custom-call | tf_op jit(solution)/shard_map/jit(cholesky)/cholesky | solution.py:119
  662.4 11.9 %cholesky.105 = f32[128,128]{1,0:T(8,128)S(1)} custom-call(f32[128,128]{1,0:T(8,128)S(1)} %convolution_subtract_fusion.3), custom_call_target="Cholesky" | custom-call | tf_op jit(solution)/shard_map/jit(cholesky)/cholesky | solution.py:119
  677.0 4.0 while.67
  681.0 19.7 %custom-call.18 = f32[2,128,128]{1,2,0:T(8,128)S(1)} custom-call(f32[2,128,128]{2,1,0:T(8,128)S(1)} %get-tuple-element.354), custom_call_target="InvertDiagBlocksLowerTriangular" | custom-call | tf_op jit(solution)/shard_map/triangular_solve | solution.py:17
  (212 shorter events, 207.7 us)
Async XLA Ops:
  7.2 430.3 %reduce-scatter.3.cloned.1.call-start = ((), (), s32[]{:S(2)}) async-start(), calls=%async_computation.2 | async-start | bytes 5242880 | tf_op jit(solution)/shard_map/reduce_scatter | solution.py:109
  15.4 6.9 copy-start.2
  15.9 2.1 copy-start
  18.0 4.2 copy-start.3
  168.3 28.2 %collective-permute-start = (f32[512,512]{0,1:T(8,128)S(1)}, f32[512,512]{0,1:T(8,128)S(1)}, u32[]{:S(2)}, u32[]{:S(2)}) collective-permute-start(f32[512,512]{0,1:T(8,128)S(1)} %slice_bitcast_fusion.1), channel_id=1, source_target_pairs={{1,0},{2,1},{3,2},{4,3},{5,4},{6,5},{7,6},{8,7},{9,8},{10,9},{11,1... | collective-permute-start | bytes 3145736 | tf_op jit(solution)/shard_map/ppermute | solution.py:13
  197.3 10.2 %copy-start.5 = (f32[1,4]{1,0:T(1,128)S(1)}, f32[1,4]{1,0:T(1,128)}, u32[]{:S(2)}) copy-start(f32[1,4]{1,0:T(1,128)} %param.23) | copy-start | bytes 52
  200.3 26.9 %collective-permute-start.1 = (f32[512,512]{0,1:T(8,128)}, f32[512,512]{0,1:T(8,128)}, u32[]{:S(2)}, u32[]{:S(2)}) collective-permute-start(f32[512,512]{0,1:T(8,128)} %convolution_bitcast_fusion.4), channel_id=1, source_target_pairs={{0,1},{1,2},{2,3},{3,4},{4,5},{5,6},{6,7},{7,8},{8,9},{9,10},{10,1... | collective-permute-start | bytes 3145736 | tf_op jit(solution)/shard_map/ppermute | solution.py:13
  212.9 14.2 %copy-start.1 = (f32[8,512,256]{1,2,0:T(8,128)S(1)}, f32[8,512,256]{1,2,0:T(8,128)}, u32[]{:S(2)}) copy-start(f32[8,512,256]{1,2,0:T(8,128)} %copy-done) | copy-start | bytes 12582916
  385.0 101.3 %reduce-scatter.5.cloned.1.call-start = ((), (), s32[]{:S(2)}) async-start(), calls=%async_computation.3 | async-start | bytes 5242880 | tf_op jit(solution)/shard_map/reduce_scatter | solution.py:110
  385.8 252.4 %all-reduce.5.cloned.1.call-start = ((), (), s32[]{:S(2)}) async-start(), calls=%async_computation.4 | async-start | bytes 1048576 | tf_op jit(solution)/shard_map/psum | solution.py:115
  437.4 52.2 %copy-start.4 = (f32[1,2,512,256]{2,3,1,0:T(8,128)S(1)}, f32[1,2,512,256]{2,3,1,0:T(8,128)}, u32[]{:S(2)}) copy-start(f32[1,2,512,256]{2,3,1,0:T(8,128)} %reduce-scatter.3.cloned.1.call-done) | copy-start | bytes 3145732
Sparse Core Ops, SparseCore 0:
  385.1 52.2 reduce-scatter.2
  440.0 46.3 reduce-scatter.4
  491.8 146.2 all-reduce.4
where the time goes:
time: 726 us; the launch traced here: 714 us
  waiting for transfers between devices  282 us (39%)
  other arithmetic  176 us (24%)
  local copies, waits for them, and re-layouts  127 us (17%)
  matrix products  99.8 us (14%)
  between operations  20.4 us (3%)
  starting transfers between devices  8.82 us (1%)
    psum x1, waiting for transfers between devices, on_device(): lax.psum((gram_part, projected_part), ('pole', 'dom'))  148 us
    dot_general x35, matrix products, complex_product(): jnp.dot(stacked, vectors.astype(jnp.bfloat16), preferred_element_type=jnp...  83.1 us
    dynamic_slice x64, local copies, waits for them, and re-layouts, partition_solve(): lax.scan(forward_step, initial, (inverse, source, previous))  82.9 us
    dynamic_update_slice x32, other arithmetic, partition_solve(): lax.scan(forward_step, initial, (inverse, source, previous))  60.9 us
    reduce_scatter x1, waiting for transfers between devices, on_device(): lax.psum_scatter(filtered_term[None], 'pole', scatter_dimension=1, tiled=...  51.5 us
    reduce_scatter x1, waiting for transfers between devices, on_device(): lax.psum_scatter(shifted_term[None], 'pole', scatter_dimension=1, tiled=T...  45.5 us
    ppermute x2, waiting for transfers between devices, shifted(): return lax.ppermute(x, axis, pairs)  36 us
    add x16, other arithmetic, backward_step(): partial_value + complex_product(block_inverse, real_product(couple_next,...  35.2 us
  transfers between devices with their start and end apart: 5, of which 5 were waited for; matrix products, arithmetic and copies ran while one was open for 1% of the time, Pallas kernels for 0%

commit v1 on v0

--- a/solution.py
+++ b/solution.py
@@ -112,7 +112,7 @@
     own_rows = owned[0].reshape(count * B, M)
     gram_part = inner_products(own_rows, own_rows)
     projected_part = inner_products(own_rows, shifted_owned[0].reshape(count * B, M))
-    gram_total, projected_total = lax.psum((gram_part, projected_part), ("pole", "dom"))
+    gram_total, projected_total = lax.psum(lax.psum((gram_part, projected_part), "pole"), "dom")
     row_total = blocks * B * lax.axis_size("dom")
     gram = gram_total / row_total
     projected = projected_total / row_total

time: 726 us -> 969 us (1.33)
  the two profiles are of different devices: /device:TPU:1 before, /device:TPU:0 now
where the time goes in v1:
time: 969 us; the launch traced here: 957 us
  waiting for transfers between devices  524 us (54%)
  other arithmetic  176 us (18%)
  local copies, waits for them, and re-layouts  127 us (13%)
  matrix products  99.8 us (10%)
  between operations  20.6 us (2%)
    psum x1, waiting for transfers between devices, on_device(): lax.psum(lax.psum((gram_part, projected_part), 'pole'), 'dom')  353 us
    dot_general x35, matrix products, complex_product(): jnp.dot(stacked, vectors.astype(jnp.bfloat16), preferred_element_type=jnp...  83.1 us
    dynamic_slice x64, local copies, waits for them, and re-layouts, partition_solve(): lax.scan(forward_step, initial, (inverse, source, previous))  82.9 us
    dynamic_update_slice x32, other arithmetic, partition_solve(): lax.scan(forward_step, initial, (inverse, source, previous))  60.9 us
    reduce_scatter x1, waiting for transfers between devices, on_device(): lax.psum_scatter(filtered_term[None], 'pole', scatter_dimension=1, tiled=...  49.6 us
    reduce_scatter x1, waiting for transfers between devices, on_device(): lax.psum_scatter(shifted_term[None], 'pole', scatter_dimension=1, tiled=T...  45.5 us
    psum x1, waiting for transfers between devices, on_device(): lax.psum((gram_part, projected_part), 'pole')  38.5 us
    ppermute x2, waiting for transfers between devices, shifted(): return lax.ppermute(x, axis, pairs)  36.5 us
  transfers between devices with their start and end apart: 6, of which 6 were waited for; matrix products, arithmetic and copies ran while one was open for 1% of the time, Pallas kernels for 0%

profile of v1, /device:TPU:0, one launch (start us, length us, event | category | flops | bytes accessed | tf_op | source)
XLA Modules:
  0.0 957.3 jit_solution(17405702631842131179)
XLA Ops:
  7.2 4.2 slice_bitcast_fusion
  12.5 2.9 copy.17
  18.0 4.2 concatenate.76
  22.3 2.3 pad_maximum_fusion.2
  24.6 4.3 broadcast.158.clone.2
  29.8 65.2 %while.65 = (s32[]{:T(128)}, bf16[512,512]{0,1:T(8,128)(2,1)}, f32[8,512,512]{1,2,0:T(8,128)}, bf16[8,2,512,512]{3,2,1,0:T(8,128)(2,1)}, f32[8,512,512]{1,2,0:T(8,128)}, /*index=5*/bf16[8,512,512]{2,1,0:T(8,128)(2,1)}, s32[]{:T(128)}) while((s32[]{:T(128)}, bf16[512,512]{0,1:T(8,128)(2,1)}, f32[8,512,512]{1,2,0:T(8,128)}, ...), condition=%wide.region_1.2_spmd, body=%wide.region_0.1_spmd.sunk | while | flops 806617088 | bytes 17302612 | solution.py:62
  33.7 2.7 fusion.131
  41.8 2.7 fusion.131
  49.9 2.7 fusion.131
  58.1 2.7 fusion.131
  66.3 2.7 fusion.131
  74.5 2.7 fusion.131
  82.6 2.7 fusion.131
  90.8 2.7 fusion.131
  95.0 4.3 broadcast.158.clone.1
  99.3 67.8 %while.68 = (s32[]{:T(128)}, bf16[512,512]{0,1:T(8,128)(2,1)}, f32[8,512,512]{1,2,0:T(8,128)}, f32[8,512,512]{1,2,0:T(8,128)}, bf16[8,2,512,512]{3,2,1,0:T(8,128...) while((s32[]{:T(128)}, bf16[512,512]{0,1:T(8,128)(2,1)}, ...), condition=%wide.region_3.4_spmd.clone, body=%wide.region_2.3_spmd.clone.sunk | while | flops 807403520 | bytes 15204483 | solution.py:69
  103.0 2.5 fusion.140
  111.6 2.4 fusion.140
  120.1 2.4 fusion.140
  128.6 2.4 fusion.140
  137.0 2.4 fusion.140
  143.0 2.3 fusion.139
  145.5 2.4 fusion.140
  154.0 2.4 fusion.140
  162.5 2.4 fusion.140
  174.0 22.8 %collective-permute-done = f32[512,512]{0,1:T(8,128)S(1)} collective-permute-done((f32[512,512]{0,1:T(8,128)S(1)}, f32[512,512]{0,1:T(8,128)S(1)}, u32[]{:S(2)}, u32[]{:S(2)}) %collective-permute-start) | collective-permute-done | bytes 1048608 | tf_op jit(solution)/shard_map/ppermute | solution.py:13
  198.0 2.5 convolution_bitcast_fusion.4
  200.5 7.5 collective-permute-start.1
  214.6 13.7 %collective-permute-done.1 = f32[512,512]{0,1:T(8,128)} collective-permute-done((f32[512,512]{0,1:T(8,128)}, f32[512,512]{0,1:T(8,128)}, u32[]{:S(2)}, u32[]{:S(2)}) %collective-permute-start.1) | collective-permute-done | bytes 1048608 | tf_op jit(solution)/shard_map/ppermute | solution.py:13
  228.3 2.3 fusion.51
  230.7 2.9 fusion.52
  233.6 4.3 broadcast.158.clone
  238.8 65.5 %while.66 = (s32[]{:T(128)}, bf16[512,512]{0,1:T(8,128)(2,1)}, f32[8,512,512]{1,2,0:T(8,128)}, bf16[8,2,512,512]{3,2,1,0:T(8,128)(2,1)}, f32[8,512,512]{1,2,0:T(8,128)}, /*index=5*/bf16[8,512,512]{2,1,0:T(8,128)(2,1)}, s32[]{:T(128)}) while((s32[]{:T(128)}, bf16[512,512]{0,1:T(8,128)(2,1)}, f32[8,512,512]{1,2,0:T(8,128)}, ...), condition=%wide.region_5.6_spmd, body=%wide.region_4.5_spmd.sunk | while | flops 806617088 | bytes 17302612 | solution.py:62
  242.7 2.7 fusion.135
  250.8 2.7 fusion.135
  259.0 2.7 fusion.135
  267.1 2.7 fusion.135
  275.4 2.7 fusion.135
  283.7 2.7 fusion.135
  291.8 2.7 fusion.135
  300.0 2.7 fusion.135
  304.3 4.3 broadcast.158
  308.6 67.7 %while.69 = (s32[]{:T(128)}, bf16[512,512]{0,1:T(8,128)(2,1)}, f32[8,512,512]{1,2,0:T(8,128)}, f32[8,512,512]{1,2,0:T(8,128)}, bf16[8,2,512,512]{3,2,1,0:T(8,128...) while((s32[]{:T(128)}, bf16[512,512]{0,1:T(8,128)(2,1)}, ...), condition=%wide.region_7.8_spmd.clone, body=%wide.region_6.7_spmd.clone.sunk | while | flops 807403520 | bytes 15204483 | solution.py:69
  312.3 2.5 fusion.144
  318.3 2.3 fusion.143
  320.9 2.4 fusion.144
  329.3 2.4 fusion.144
  337.8 2.4 fusion.144
  346.3 2.4 fusion.144
  354.8 2.4 fusion.144
  363.2 2.4 fusion.144
  371.7 2.4 fusion.144
  376.3 10.0 %subtract_bitcast_fusion = (f32[1,8,512,256]{2,3,1,0:T(8,128)}, f32[1,8,512,256]{2,3,1,0:T(8,128)}) fusion(f32[8,512,512]{1,2,0:T(8,128)} %get-tuple-element.338, f32[]{:T(128)S(6)} %add.173, f32[]{:T(128)S(6)} %sub.71, f32[]{:T(128)} %bitcast.8, bf16[1,8,512,256]{2,3,1,0:T(8,128)(2,1)} %copy-done.2, f32[]{:T(128)} %bitcast.27), kind=kLoop, calls=%fused_computation.61 | loop fusion | flops 9437184 | bytes 18874384 | tf_op jit(solution)/shard_map/broadcast_in_dim | solution.py:110
  387.1 49.6 %reduce-scatter.3.cloned.1.call-done = f32[1,2,512,256]{2,3,1,0:T(8,128)} async-done(((f32[1,8,512,256]{2,3,1,0:T(8,128)}), f32[1,2,512,256]{2,3,1,0:T(8,128)}) %reduce-scatter.3.cloned.1.call-update) | async-done | bytes 1048592 | tf_op jit(solution)/shard_map/reduce_scatter | solution.py:109
  436.7 3.4 convolution_bitcast_fusion.6
  440.1 45.5 %reduce-scatter.5.cloned.1.call-done = f32[1,2,512,256]{2,3,1,0:T(8,128)} async-done(((f32[1,8,512,256]{2,3,1,0:T(8,128)}), f32[1,2,512,256]{2,3,1,0:T(8,128)}) %reduce-scatter.5.cloned.1.call-update) | async-done | bytes 1048592 | tf_op jit(solution)/shard_map/reduce_scatter | solution.py:110
  485.6 3.3 convolution_bitcast_fusion.5
  489.1 38.5 %all-reduce.9.cloned.1.call-done = (f32[256,256]{0,1:T(8,128)}, f32[256,256]{0,1:T(8,128)}) async-done(((f32[256,256]{0,1:T(8,128)}, f32[256,256]{0,1:T(8,128)}), (f32[256,256]{0,1:T(8,128)}, f32[256,256]{0,1:T(8,128)})) %all-reduce.9.cloned.1.call-update) | async-done | bytes 524304 | tf_op jit(solution)/shard_map/psum | solution.py:115
  528.0 353.3 %all-reduce.7.cloned.1.call-done = (f32[256,256]{0,1:T(8,128)}, f32[256,256]{0,1:T(8,128)}) async-done(((f32[256,256]{0,1:T(8,128)}, f32[256,256]{0,1:T(8,128)}), (f32[256,256]{0,1:T(8,128)}, f32[256,256]{0,1:T(8,128)})) %all-reduce.7.cloned.1.call-update) | async-done | bytes 524304 | tf_op jit(solution)/shard_map/psum | solution.py:115
  883.5 11.7 %cholesky.50 = f32[128,128]{1,0:T(8,128)S(1)} custom-call(f32[128,128]{1,0:T(8,128)S(1)} %cholesky.118), custom_call_target="Cholesky" | custom-call | tf_op jit(solution)/shard_map/jit(cholesky)/cholesky | solution.py:119
  895.2 9.8 %custom-call.17 = f32[1,128,128]{1,2,0:T(8,128)S(1)} custom-call(f32[1,128,128]{2,1,0:T(8,128)S(1)} %get-tuple-element.521), custom_call_target="InvertDiagBlocksLowerTriangular" | custom-call | tf_op jit(solution)/shard_map/jit(cholesky)/cholesky | solution.py:119
  905.5 11.7 %cholesky.105 = f32[128,128]{1,0:T(8,128)S(1)} custom-call(f32[128,128]{1,0:T(8,128)S(1)} %convolution_subtract_fusion.3), custom_call_target="Cholesky" | custom-call | tf_op jit(solution)/shard_map/jit(cholesky)/cholesky | solution.py:119
  920.0 4.2 while.67
  924.2 19.7 %custom-call.18 = f32[2,128,128]{1,2,0:T(8,128)S(1)} custom-call(f32[2,128,128]{2,1,0:T(8,128)S(1)} %get-tuple-element.354), custom_call_target="InvertDiagBlocksLowerTriangular" | custom-call | tf_op jit(solution)/shard_map/triangular_solve | solution.py:17
  (215 shorter events, 210.4 us)
Async XLA Ops:
  7.2 429.5 %reduce-scatter.3.cloned.1.call-start = ((), (), s32[]{:S(2)}) async-start(), calls=%async_computation.2 | async-start | bytes 5242880 | tf_op jit(solution)/shard_map/reduce_scatter | solution.py:109
  15.4 6.9 copy-start.2
  16.0 2.1 copy-start
  18.0 4.3 copy-start.3
  168.4 28.3 %collective-permute-start = (f32[512,512]{0,1:T(8,128)S(1)}, f32[512,512]{0,1:T(8,128)S(1)}, u32[]{:S(2)}, u32[]{:S(2)}) collective-permute-start(f32[512,512]{0,1:T(8,128)S(1)} %slice_bitcast_fusion.1), channel_id=1, source_target_pairs={{1,0},{2,1},{3,2},{4,3},{5,4},{6,5},{7,6},{8,7},{9,8},{10,9},{11,1... | collective-permute-start | bytes 3145736 | tf_op jit(solution)/shard_map/ppermute | solution.py:13
  197.5 10.5 %copy-start.5 = (f32[1,4]{1,0:T(1,128)S(1)}, f32[1,4]{1,0:T(1,128)}, u32[]{:S(2)}) copy-start(f32[1,4]{1,0:T(1,128)} %param.23) | copy-start | bytes 52
  200.5 27.8 %collective-permute-start.1 = (f32[512,512]{0,1:T(8,128)}, f32[512,512]{0,1:T(8,128)}, u32[]{:S(2)}, u32[]{:S(2)}) collective-permute-start(f32[512,512]{0,1:T(8,128)} %convolution_bitcast_fusion.4), channel_id=1, source_target_pairs={{0,1},{1,2},{2,3},{3,4},{4,5},{5,6},{6,7},{7,8},{8,9},{9,10},{10,1... | collective-permute-start | bytes 3145736 | tf_op jit(solution)/shard_map/ppermute | solution.py:13
  213.6 14.7 %copy-start.1 = (f32[8,512,256]{1,2,0:T(8,128)S(1)}, f32[8,512,256]{1,2,0:T(8,128)}, u32[]{:S(2)}) copy-start(f32[8,512,256]{1,2,0:T(8,128)} %copy-done) | copy-start | bytes 12582916
  386.3 99.3 %reduce-scatter.5.cloned.1.call-start = ((), (), s32[]{:S(2)}) async-start(), calls=%async_computation.3 | async-start | bytes 5242880 | tf_op jit(solution)/shard_map/reduce_scatter | solution.py:110
  387.1 140.5 %all-reduce.9.cloned.1.call-start = ((), (), s32[]{:S(2)}) async-start(), calls=%async_computation.5 | async-start | bytes 1048576 | tf_op jit(solution)/shard_map/psum | solution.py:115
  436.7 90.9 %copy-start.4 = (f32[1,2,512,256]{2,3,1,0:T(8,128)S(1)}, f32[1,2,512,256]{2,3,1,0:T(8,128)}, u32[]{:S(2)}) copy-start(f32[1,2,512,256]{2,3,1,0:T(8,128)} %reduce-scatter.3.cloned.1.call-done) | copy-start | bytes 3145732
  488.9 392.4 %all-reduce.7.cloned.1.call-start = ((), (), s32[]{:S(2)}) async-start(), calls=%async_computation.4 | async-start | bytes 1048576 | tf_op jit(solution)/shard_map/psum | solution.py:115
Sparse Core Ops, SparseCore 0:
  386.5 50.2 reduce-scatter.2
  439.2 46.3 reduce-scatter.4
  489.0 38.5 all-reduce.8
  530.0 351.2 all-reduce.6
